TPU v7x, 512 devices: a whole 4x8x8 slice. The times are simulated.
512 devices in a mesh: dp: 2 (over y_hi), row: 16 (over z, core), col: 16 (over x, y_lo).
Axes of the slice: x: 4, y: 8 (y_hi: 2, y_lo: 4; y = y_hi * 4 + y_lo), z: 8, core: 2. Of those that a mesh axis runs over, the one named last changes fastest.
Arguments:
- inputs: bfloat16 [4096, 6144], P(('dp', 'row'), 'col'), may hold values from -6 to 6
- gain: float32 [6144], P('row'), may hold values from 0.4 to 1.6
- w_in: bfloat16 [6144, 24576], P('row', 'col'), may hold values from -0.078125 to 0.078125
- pre_act: bfloat16 [4096, 24576], P(('dp', 'row'), 'col'), may hold values from -6 to 6
- grad_act: bfloat16 [4096, 24576], P(('dp', 'row'), 'col'), may hold values from -6 to 6
Outputs:
- grad_input: bfloat16 [4096, 6144], P(('dp', 'col'), 'row')
- grad_w_in: float32 [6144, 24576], P('row', 'col')
- grad_gain: float32 [6144], P('row')
All inputs are finite; a program needn't handle non-finite values.
Results may differ from a plain program's by a relative error of at most 0.0049.
Values may be sent and summed in bfloat16 or wider, within the bound.
A program may use at most 64 MiB of HBM per device.

v0:
```python
import math

import jax
import jax.numpy as jnp
from jax import lax
from jax.sharding import PartitionSpec as P

epsilon = 1e-06


def spread(block, axis, owner):
    block = jnp.where(lax.axis_index(axis) == owner, block, jnp.zeros_like(block))
    return lax.psum(block, axis)


def gelu_slope(values):
    coeff = math.sqrt(2.0 / math.pi)
    inner = coeff * (values + 0.044715 * values * values * values)
    tangent = jnp.tanh(inner)
    return 0.5 * (1.0 + tangent) + 0.5 * values * (1.0 - tangent * tangent) * coeff * (
        1.0 + 3.0 * 0.044715 * values * values
    )


def shards(inputs, gain, w_in, pre_act, grad_act):
    own_rows = inputs.shape[0]
    slopes = gelu_slope(pre_act.astype(jnp.float32))
    act_grad = (grad_act.astype(jnp.float32) * slopes).astype(jnp.bfloat16)
    act_rows = lax.all_gather(act_grad, "row", axis=0, tiled=True)
    stacked = lax.all_gather(inputs, "row", axis=0, tiled=True)
    columns = spread(stacked, "col", lax.axis_index("row"))
    values = columns.astype(jnp.float32)
    features = gain.shape[0] * lax.axis_size("row")
    moment_sums = lax.psum((jnp.sum(values, axis=1), jnp.sum(values * values, axis=1)), "row")
    row_mean = moment_sums[0] / features
    variance = moment_sums[1] / features - row_mean * row_mean
    inv_std = lax.rsqrt(variance + epsilon)
    normed = (values - row_mean[:, None]) * inv_std[:, None]
    hidden = (normed * gain[None, :]).astype(jnp.bfloat16)
    local_grad = lax.dot_general(
        hidden, act_rows, (((0,), (0,)), ((), ())), preferred_element_type=jnp.float32
    )
    grad_w_in = lax.psum(local_grad, "dp")
    grad_hidden = lax.psum_scatter(
        lax.dot_general(
            act_rows, w_in, (((1,), (1,)), ((), ())), preferred_element_type=jnp.float32
        ),
        "col",
        scatter_dimension=0,
        tiled=True,
    )
    first_own = lax.axis_index("col") * own_rows
    own_normed = lax.dynamic_slice_in_dim(normed, first_own, own_rows, 0)
    own_inv_std = lax.dynamic_slice_in_dim(inv_std, first_own, own_rows, 0)
    scaled = grad_hidden * gain[None, :]
    row_sums = lax.psum((jnp.sum(scaled, axis=1), jnp.sum(scaled * own_normed, axis=1)), "row")
    first_mean = row_sums[0] / features
    second_mean = row_sums[1] / features
    grad_input = (
        own_inv_std[:, None] * (scaled - first_mean[:, None] - own_normed * second_mean[:, None])
    ).astype(jnp.bfloat16)
    grad_gain = lax.psum(jnp.sum(grad_hidden * own_normed, axis=0), ("dp", "col"))
    return (grad_input, grad_w_in, grad_gain)


def solution(mesh):
    return jax.shard_map(
        shards,
        mesh=mesh,
        in_specs=(
            P(("dp", "row"), "col"),
            P("row"),
            P("row", "col"),
            P(("dp", "row"), "col"),
            P(("dp", "row"), "col"),
        ),
        out_specs=(P(("dp", "col"), "row"), P("row", "col"), P("row")),
        check_vma=False,
    )
```

profile of v0, /device:TPU:1, one launch (start us, length us, event | category | flops | bytes accessed | tf_op | source)
XLA Modules:
  0.0 537.2 jit_solution(8824059350542461723)
XLA Ops:
  7.2 0.0 copy-start
  7.2 0.0 all-gather.3.cloned.1.call-start
  7.2 0.7 all-gather.3.cloned.1.call-update
  7.9 0.0 all-gather.5.cloned.1.call-start
  8.0 2.4 fusion.11
  10.4 0.0 all-gather.5.cloned.1.call-update
  10.4 0.0 all-reduce.5.cloned.1.call-start
  10.5 48.2 %all-gather.3.cloned.1.call-done = bf16[2048,384]{1,0:T(8,128)(2,1)} async-done(((bf16[128,384]{1,0:T(8,128)(2,1)}), bf16[2048,384]{1,0:T(8,128)(2,1)}) %all-gather.3.cloned.1.call-update) | async-done | bytes 1572880 | tf_op jit(solution)/shard_map/all_gather | solution.py:30
  58.6 1.3 broadcast_select_fusion
  59.9 0.0 all-reduce.5.cloned.1.call-update
  60.0 0.0 reduce-scatter.2.cloned.1.call-start
  60.0 48.3 %all-gather.5.cloned.1.call-done = bf16[2048,1536]{1,0:T(8,128)(2,1)} async-done(((bf16[128,1536]{1,0:T(8,128)(2,1)}), bf16[2048,1536]{1,0:T(8,128)(2,1)}) %all-gather.5.cloned.1.call-update) | async-done | bytes 6291472 | tf_op jit(solution)/shard_map/all_gather | solution.py:29
  108.3 0.0 copy-done
  108.3 7.9 %fusion.14 = f32[2048,384]{1,0:T(8,128)} fusion(bf16[2048,1536]{1,0:T(8,128)(2,1)} %all-gather.5.cloned.1.call-done, bf16[384,1536]{1,0:T(8,128)(2,1)S(1)} %copy-done), kind=kOutput, calls=%fused_computation.33 | convolution fusion | flops 2415919104 | bytes 10616832 | tf_op jit(solution)/shard_map/dot_general | solution.py:45
  116.2 0.0 copy-start.2
  116.2 0.0 reduce-scatter.2.cloned.1.call-update
  116.3 0.0 all-reduce.7.cloned.1.call-start
  116.3 159.8 %all-reduce.5.cloned.1.call-done = bf16[2048,384]{1,0:T(8,128)(2,1)} async-done(((bf16[2048,384]{1,0:T(8,128)(2,1)}), bf16[2048,384]{1,0:T(8,128)(2,1)}) %all-reduce.5.cloned.1.call-update) | async-done | bytes 1572880 | tf_op jit(solution)/shard_map/psum | solution.py:13
  276.1 2.0 convert_reduce_fusion
  278.2 54.7 %all-reduce.1 = (f32[2048]{0:T(1024)S(1)}, f32[2048]{0:T(1024)S(1)}) all-reduce(f32[2048]{0:T(1024)S(1)} %get-tuple-element.6, f32[2048]{0:T(1024)S(1)} %get-tuple-element.5), channel_id=1, replica_groups=mesh['dp'=2,'row'=16,'col'=16] {'row'}, use_global_device_ids=true, to_apply=%region_2.3 | all-reduce | flops 4096 | bytes 32768 | tf_op jit(solution)/shard_map/psum | solution.py:34
  332.8 0.0 copy-done.2
  332.8 7.5 %fusion.2 = f32[384,1536]{1,0:T(8,128)} fusion(bf16[2048,1536]{1,0:T(8,128)(2,1)} %all-gather.5.cloned.1.call-done, f32[384]{0:T(512)S(1)} %copy-done.2, bf16[2048,384]{1,0:T(8,128)(2,1)} %all-reduce.5.cloned.1.call-done, f32[2048]{0:T(1024)S(1)} %get-tuple-element.13, f32[2048]{0:T(1024)S(1)} %get-tuple-element.12), kind=kOutput, calls=%fused_computation.13 | convolution fusion | flops 2419851264 | bytes 10241536 | tf_op jit(solution)/shard_map/dot_general | solution.py:40
  340.3 0.0 copy-start.1
  340.3 0.0 all-reduce.7.cloned.1.call-update
  340.4 0.1 dynamic_slice.6
  340.4 1.3 copy-done.1
  341.8 2.0 fusion.1
  343.8 31.8 %reduce-scatter.2.cloned.1.call-done = f32[128,384]{1,0:T(8,128)} async-done(((f32[2048,384]{1,0:T(8,128)}), f32[128,384]{1,0:T(8,128)}) %reduce-scatter.2.cloned.1.call-update) | async-done | bytes 196624 | tf_op jit(solution)/shard_map/reduce_scatter | solution.py:44
  375.5 1.1 multiply_reduce_fusion
  376.6 34.0 %all-reduce = (f32[128]{0:T(128)S(1)}, f32[128]{0:T(128)S(1)}) all-reduce(f32[128]{0:T(128)S(1)} %get-tuple-element.4, f32[128]{0:T(128)S(1)} %get-tuple-element.7), channel_id=1, replica_groups=mesh['dp'=2,'row'=16,'col'=16] {'row'}, use_global_device_ids=true, to_apply=%region_9.10 | all-reduce | flops 256 | bytes 2048 | tf_op jit(solution)/shard_map/psum | solution.py:56
  410.7 87.9 %psum.55 = f32[384]{0:T(512)} all-reduce(f32[384]{0:T(512)S(1)} %get-tuple-element.3), channel_id=1, replica_groups=mesh['dp'=2,'row'=16,'col'=16] {'dp','col'}, use_global_device_ids=true, to_apply=%region_12.13 | all-reduce | flops 384 | bytes 3072 | tf_op jit(solution)/shard_map/psum | solution.py:62
  498.6 1.8 multiply_convert_fusion.2
  500.4 27.1 %all-reduce.7.cloned.1.call-done = f32[384,1536]{1,0:T(8,128)} async-done(((f32[384,1536]{1,0:T(8,128)}), f32[384,1536]{1,0:T(8,128)}) %all-reduce.7.cloned.1.call-update) | async-done | bytes 2359312 | tf_op jit(solution)/shard_map/psum | solution.py:43
  527.4 3.2 copy.10
  (2 shorter events, 0.0 us)
Async XLA Ops:
  7.2 101.1 %copy-start = (bf16[384,1536]{1,0:T(8,128)(2,1)S(1)}, bf16[384,1536]{1,0:T(8,128)(2,1)}, u32[]{:S(2)}) copy-start(bf16[384,1536]{1,0:T(8,128)(2,1)} %param.7) | copy-start | bytes 3538948
  7.2 51.5 %all-gather.3.cloned.1.call-start = ((), (), s32[]{:S(2)}) async-start(), calls=%async_computation.1 | async-start | bytes 1671168 | tf_op jit(solution)/shard_map/all_gather | solution.py:30
  7.9 100.4 %all-gather.5.cloned.1.call-start = ((), (), s32[]{:S(2)}) async-start(), calls=%async_computation.3 | async-start | bytes 6684672 | tf_op jit(solution)/shard_map/all_gather | solution.py:29
  10.4 265.7 %all-reduce.5.cloned.1.call-start = ((), (), s32[]{:S(2)}) async-start(), calls=%async_computation.2 | async-start | bytes 3145728 | tf_op jit(solution)/shard_map/psum | solution.py:13
  60.0 315.5 %reduce-scatter.2.cloned.1.call-start = ((), (), s32[]{:S(2)}) async-start(), calls=%async_computation.4 | async-start | bytes 3342336 | tf_op jit(solution)/shard_map/reduce_scatter | solution.py:44
  116.2 216.6 %copy-start.2 = (f32[384]{0:T(512)S(1)}, f32[384]{0:T(512)}, u32[]{:S(2)}) copy-start(f32[384]{0:T(512)} %param.6) | copy-start | bytes 4612
  116.3 411.2 %all-reduce.7.cloned.1.call-start = ((), (), s32[]{:S(2)}) async-start(), calls=%async_computation.5 | async-start | bytes 4718592 | tf_op jit(solution)/shard_map/psum | solution.py:43
  340.3 1.4 copy-start.1
Sparse Core Ops, SparseCore 0:
  10.1 48.4 all-gather.2
  60.8 47.4 all-gather.4
  111.8 164.2 all-reduce.4
  279.1 96.3 reduce-scatter.1
  379.1 148.3 all-reduce.6
where the time goes:
time: 541 us; the launch traced here: 537 us
  waiting for transfers between devices  316 us (58%)
  blocking collectives  177 us (33%)
  matrix products  15.4 us (3%)
  between operations  13.8 us (3%)
  other arithmetic  10.7 us (2%)
    psum x1, waiting for transfers between devices, spread(): return lax.psum(block, axis)  160 us
    psum x1, blocking collectives, shards(): lax.psum(jnp.sum(grad_hidden * own_normed, axis=0), ('dp', 'col'))  87.9 us
    psum x1, blocking collectives, shards(): lax.psum((jnp.sum(values, axis=1), jnp.sum(values * values, axis=1)), 'row')  54.7 us
    all_gather x1, waiting for transfers between devices, shards(): act_rows = lax.all_gather(act_grad, 'row', axis=0, tiled=True)  48.3 us
    all_gather x1, waiting for transfers between devices, shards(): stacked = lax.all_gather(inputs, 'row', axis=0, tiled=True)  48.2 us
    psum x1, blocking collectives, shards(): lax.psum((jnp.sum(scaled, axis=1), jnp.sum(scaled * own_normed, axis=1)),...  34 us
    reduce_scatter x1, waiting for transfers between devices, shards(): lax.psum_scatter(lax.dot_general(act_rows, w_in, (((1,), (1,)), ((), ()))...  31.8 us
    psum x1, waiting for transfers between devices, shards(): grad_w_in = lax.psum(local_grad, 'dp')  27.1 us
  transfers between devices with their start and end apart: 5, of which 5 were waited for; matrix products, arithmetic and copies ran while one was open for 5% of the time, Pallas kernels for 0%

commit v1 on v0

v1 whole, which is shorter than its diff:
```python
import math

import jax
import jax.numpy as jnp
from jax import lax
from jax.experimental import pallas as pl
from jax.experimental.pallas import tpu as pltpu
from jax.sharding import PartitionSpec as P

MESH = pl.DeviceIdType.MESH
EPSILON = 1e-06
ROWS = 128
FEAT = 384
UNITS = 1536
NZ, NX, NY = 8, 4, 8
FEATURES = 6144.0
CH = 2
CROWS = ROWS // CH
F32 = jnp.float32
BF16 = jnp.bfloat16
HIGH = lax.Precision.HIGHEST


def gelu_slope(values):
    coeff = math.sqrt(2.0 / math.pi)
    inner = coeff * (values + 0.044715 * values * values * values)
    tangent = jnp.tanh(inner)
    return 0.5 * (1.0 + tangent) + 0.5 * values * (1.0 - tangent * tangent) * coeff * (
        1.0 + 3.0 * 0.044715 * values * values
    )


def kernel(
    x_ref, gain_ref, w_ref, pre_ref, ga_ref,
    gi_ref, gw_ref, gg_ref,
    act, hid, acc, wt, part, rx, own, ty, ry, xin, normed, st1, st2, gy, gx,
    xt_send, xt_recv, act_recv, ring_send, sib_send, dp_send,
    h_recv, hy_send, hx_send, s1_send, s1_recv, s2_send, s2_recv,
    rx_send, rx_recv, ry_send, ry_recv, gy_send, gy_recv, gx_send, gx_recv,
):
    d, r, c = lax.axis_index("dp"), lax.axis_index("row"), lax.axis_index("col")
    z, k = r // 2, r % 2
    x, y = c // 4, c % 4
    yy = d * 4 + y

    def at(dp=None, row=None, col=None):
        return {
            "dp": d if dp is None else dp,
            "row": r if row is None else row,
            "col": c if col is None else col,
        }

    def at_z(zz):
        return at(row=zz * 2 + k)

    def at_y(big):
        return at(dp=big // 4, col=x * 4 + big % 4)

    def at_x(xx):
        return at(col=xx * 4 + y)

    def remote(src, dst, send, recv, device):
        return pltpu.make_async_remote_copy(
            src_ref=src, dst_ref=dst, send_sem=send, recv_sem=recv,
            device_id=device, device_id_type=MESH,
        )

    sibling = at(row=z * 2 + 1 - k)
    zm = lambda s: (z + s + NZ) % NZ
    ym = lambda s: (yy + s + NY) % NY
    xm = lambda s: (x + s + NX) % NX

    barrier = pltpu.get_barrier_semaphore()

    def greet(device):
        pl.semaphore_signal(barrier, inc=1, device_id=device, device_id_type=MESH)

    @pl.loop(1, 16)
    def _(i):
        greet(at(row=(r + i) % 16))

    @pl.loop(1, NY)
    def _(i):
        greet(at_y((yy + i) % NY))

    @pl.loop(1, NX)
    def _(i):
        greet(at_x((x + i) % NX))

    @pl.when(r != c)
    def _():
        greet(at(row=c, col=r))

    @pl.when(r != c)
    def _():
        pl.semaphore_wait(barrier, 15 + NY - 1 + NX - 1 + 1)

    @pl.when(r == c)
    def _():
        pl.semaphore_wait(barrier, 15 + NY - 1 + NX - 1)

    swap = remote(x_ref, xin, xt_send, xt_recv, at(row=c, col=r))

    @pl.when(r != c)
    def _():
        swap.start()

    @pl.when(r == c)
    def _():
        xin[...] = x_ref[...]

    def act_piece(ph, zz, kk, ch):
        return act.at[ph, zz, pl.ds(pl.multiple_of(kk * ROWS + ch * CROWS, CROWS), CROWS), :]

    def ring_copy(ph, zz, ch, to, slot):
        piece = act_piece(ph, zz, k, ch)
        return remote(
            piece, piece, ring_send.at[ph, slot, ch], act_recv.at[ph, zz, k, ch], at_z(to)
        )

    def sib_copy(ph, zz, kk, ch, slot):
        piece = act_piece(ph, zz, kk, ch)
        return remote(
            piece, piece, sib_send.at[ph, slot, ch], act_recv.at[ph, zz, kk, ch], sibling
        )

    def dp_copy(ch):
        return remote(
            act_piece(0, z, k, ch), act_piece(1, z, k, ch),
            dp_send.at[ch], act_recv.at[1, z, k, ch], at(dp=1 - d),
        )

    def wait_act(ph, zz, kk, ch):
        sib_copy(ph, zz, kk, ch, 0).wait_recv()

    def start_own(ph, ch):
        ring_copy(ph, z, ch, zm(1), 0).start()
        ring_copy(ph, z, ch, zm(-1), 1).start()
        sib_copy(ph, z, k, ch, 0).start()

    for ch in range(CH):
        @pl.loop(0, CROWS // 16)
        def _(i):
            here = pl.ds(pl.multiple_of(ch * CROWS + i * 16, 16), 16)
            there = pl.ds(pl.multiple_of(k * ROWS + ch * CROWS + i * 16, 16), 16)
            slopes = gelu_slope(pre_ref[here, :].astype(F32))
            act[0, z, there, :] = (ga_ref[here, :].astype(F32) * slopes).astype(BF16)

        start_own(0, ch)
        dp_copy(ch).start()

    def ring_step(ph, s):
        for ch in range(CH):
            if s < 4:
                for sign, slot in ((-1, 0), (1, 1)):
                    zz = zm(sign * s)
                    wait_act(ph, zz, k, ch)
                    if s < 3:
                        ring_copy(ph, zz, ch, zm(-sign), 2 * s + slot).start()
                    sib_copy(ph, zz, k, ch, 2 * s - 1 + slot).start()
                if s == 3:
                    sign = 2 * k - 1
                    ring_copy(ph, zm(sign * 3), ch, zm(-sign), 6).start()
            else:
                zz = zm(4)
                wait_act(ph, zz, k, ch)
                sib_copy(ph, zz, k, ch, 7).start()

    def wait_sibling(ph, zz):
        for ch in range(CH):
            wait_act(ph, zz, 1 - k, ch)

    @pl.when(r != c)
    def _():
        swap.wait_recv()

    ones = jnp.ones((8, FEAT), F32)
    first_row = lax.broadcasted_iota(jnp.int32, (8, ROWS), 0) == 0

    def row_pair(a, b):
        dims = (((1,), (1,)), ((), ()))
        sum_a = lax.dot_general(ones, a, dims, precision=HIGH, preferred_element_type=F32)
        sum_b = lax.dot_general(ones, b, dims, precision=HIGH, preferred_element_type=F32)
        return jnp.where(first_row, sum_a, sum_b)

    def stat_copy(buf, send, recv, i):
        return remote(buf.at[r], buf.at[r], send.at[i], recv.at[r], at(row=(r + i) % 16))

    def stat_start(buf, send, recv):
        @pl.loop(1, 16)
        def _(i):
            stat_copy(buf, send, recv, i).start()

    def stat_finish(buf, send, recv):
        @pl.loop(1, 16)
        def _(i):
            other = (r + i) % 16
            remote(buf.at[other], buf.at[other], send.at[i], recv.at[other], sibling).wait_recv()

        total = buf[0]
        for i in range(1, 16):
            total = total + buf[i]
        column = jnp.concatenate([total] * 16, axis=0).T / FEATURES
        return column[:, 0:1], column[:, 1:2]

    values = xin[...].astype(F32)
    st1[r] = row_pair(values, values * values)
    stat_start(st1, s1_send, s1_recv)

    @pl.loop(0, UNITS // 128)
    def _(i):
        span = pl.ds(pl.multiple_of(i * 128, 128), 128)
        wt[span, :] = w_ref[:, span].T

    def grad_hidden_part(zz):
        wait_sibling(0, zz)
        half = pl.ds(pl.multiple_of((zz % 2) * 256, 256), 256)
        part[zz // 2, half, :] = jnp.dot(
            act[0, zz], wt[...], preferred_element_type=F32
        ).astype(BF16)

    grad_hidden_part(z)

    row_mean, square_mean = stat_finish(st1, s1_send, s1_recv)
    variance = square_mean - row_mean * row_mean
    inv_std = lax.rsqrt(variance + EPSILON)
    normed[...] = (values - row_mean) * inv_std
    hidden = normed[...] * gain_ref[...]
    hid[d * 16 + c] = hidden.T.astype(BF16)

    def hid_copy(block, device, send):
        return remote(hid.at[block], hid.at[block], send, h_recv.at[block], device)

    def hid_block(big, xx):
        return (big // 4) * 16 + xx * 4 + big % 4

    def hid_to_x(big, slot):
        block = hid_block(big, x)
        hid_copy(block, at_x(xm(1)), hx_send.at[3 * slot]).start()
        hid_copy(block, at_x(xm(-1)), hx_send.at[3 * slot + 1]).start()

    def wait_hid(block):
        hid_copy(block, sibling, hx_send.at[0]).wait_recv()

    def hid_y_step(s):
        if s < 4:
            for sign, slot in ((-1, 0), (1, 1)):
                big = ym(sign * s)
                wait_hid(hid_block(big, x))
                if s < 3:
                    hid_copy(hid_block(big, x), at_y(ym(-sign)), hy_send.at[2 * s + slot]).start()
                hid_to_x(big, 2 * s - 1 + slot)
            if s == 3:
                sign = 2 * k - 1
                hid_copy(hid_block(ym(3 * sign), x), at_y(ym(-sign)), hy_send.at[6]).start()
        else:
            big = ym(4)
            wait_hid(hid_block(big, x))
            hid_to_x(big, 7)

    def y_of(slot):
        if slot == 0:
            return yy
        if slot == 7:
            return ym(4)
        return ym((1, -1)[slot % 2] * ((slot + 1) // 2))

    def hid_x_step(slot):
        big = y_of(slot)
        wait_hid(hid_block(big, xm(1)))
        wait_hid(hid_block(big, xm(-1)))
        sign = 2 * k - 1
        hid_copy(hid_block(big, xm(sign)), at_x(xm(-sign)), hx_send.at[3 * slot + 2]).start()

    for sign, slot in ((1, 0), (-1, 1)):
        hid_copy(hid_block(yy, x), at_y(ym(sign)), hy_send.at[slot]).start()
    hid_to_x(yy, 0)

    def rx_copy(j, i):
        return remote(part.at[j], rx.at[x], rx_send.at[i], rx_recv.at[x], at_x(j))

    def rx_start(j, i):
        @pl.when(j != x)
        def _():
            rx_copy(j, i).start()

    even = 1 - z % 2
    group = (
        z // 2,
        (z // 2 + 4 + 1 - 2 * even) % 4,
        (z // 2 + 4 - 1 + 2 * even) % 4,
        (z // 2 + 2) % 4,
    )

    ring_step(0, 1)
    hid_y_step(1)
    grad_hidden_part(zm(1))
    hid_y_step(2)
    grad_hidden_part(zm(-1))
    rx_start(group[0], 0)
    hid_x_step(0)

    ring_step(0, 2)
    hid_y_step(3)
    hid_x_step(1)
    hid_x_step(2)
    grad_hidden_part(zm(2))
    hid_y_step(4)
    grad_hidden_part(zm(-2))
    rx_start(group[1], 1)
    hid_x_step(3)
    hid_x_step(4)

    ring_step(0, 3)
    for ch in range(CH):
        wait_act(1, z, k, ch)
        start_own(1, ch)
    grad_hidden_part(zm(3))
    hid_x_step(5)
    grad_hidden_part(zm(-3))
    rx_start(group[2], 2)
    hid_x_step(6)
    hid_x_step(7)

    ring_step(0, 4)
    grad_hidden_part(zm(4))
    rx_start(group[3], 3)

    def project(ph, zz, first=False):
        replica = d if ph == 0 else 1 - d
        lhs = jnp.concatenate(
            [hid[replica * 16 + 2 * zz], hid[replica * 16 + 2 * zz + 1]], axis=1
        )

        @pl.loop(0, UNITS // 512)
        def _(i):
            span = pl.ds(pl.multiple_of(i * 512, 512), 512)
            term = jnp.dot(lhs, act[ph, zz, :, span], preferred_element_type=F32)
            out = gw_ref if ph == 0 else acc
            if first:
                out[:, span] = term
            else:
                out[:, span] = out[:, span] + term

    @pl.loop(0, 8)
    def _(slot):
        big = (yy + slot) % NY
        wait_hid(hid_block(big, xm(2)))

    for s in (0, 1, -1, 2):
        project(0, zm(s), first=s == 0)

    ring_step(1, 1)

    for s in (-2, 3, -3, 4):
        project(0, zm(s))

    @pl.loop(1, NX)
    def _(i):
        other = (x + i) % NX
        remote(part.at[0], rx.at[other], rx_send.at[0], rx_recv.at[other], sibling).wait_recv()

    def x_sum(yq):
        rows = pl.ds(pl.multiple_of(yq * ROWS, ROWS), ROWS)
        total = part[x, rows, :].astype(F32)
        for i in range(1, NX):
            total = total + rx[xm(i), rows, :].astype(F32)
        return total

    def ry_copy(i):
        to = (y + i) % 4
        return remote(ty.at[to], ry.at[y], ry_send.at[i], ry_recv.at[y], at(col=x * 4 + to))

    for i in range(1, 4):
        ty[(y + i) % 4] = x_sum((y + i) % 4).astype(BF16)
        ry_copy(i).start()
    own[...] = x_sum(y)

    wait_sibling(1, z)
    project(1, z, first=True)
    ring_step(1, 2)

    for i in range(1, 4):
        other = (y + i) % 4
        remote(ty.at[0], ry.at[other], ry_send.at[0], ry_recv.at[other], sibling).wait_recv()
    grad_hidden = own[...]
    for i in range(1, 4):
        grad_hidden = grad_hidden + ry[(y + i) % 4].astype(F32)

    scaled = grad_hidden * gain_ref[...]
    own_normed = normed[...]
    st2[r] = row_pair(scaled, scaled * own_normed)
    stat_start(st2, s2_send, s2_recv)
    own[...] = scaled

    def gain_sum(buf, count, me, send, recv, device_of):
        @pl.loop(1, count)
        def _(i):
            remote(buf.at[me], buf.at[me], send.at[i], recv.at[me], device_of((me + i) % count)).start()

    def gain_wait(buf, count, me, send, recv):
        @pl.loop(1, count)
        def _(i):
            other = (me + i) % count
            remote(buf.at[other], buf.at[other], send.at[i], recv.at[other], sibling).wait_recv()

        total = buf[0]
        for i in range(1, count):
            total = total + buf[i]
        return total

    def gain_drain(buf, count, me, send, recv):
        @pl.loop(1, count)
        def _(i):
            remote(buf.at[me], buf.at[me], send.at[i], recv.at[me], sibling).wait_send()

    gy[yy] = jnp.broadcast_to(
        jnp.sum(grad_hidden * own_normed, axis=0, keepdims=True), (8, FEAT)
    )
    gain_sum(gy, NY, yy, gy_send, gy_recv, at_y)

    for s in (1, -1):
        wait_sibling(1, zm(s))
        project(1, zm(s))

    gx[x] = gain_wait(gy, NY, yy, gy_send, gy_recv)
    gain_sum(gx, NX, x, gx_send, gx_recv, at_x)
    ring_step(1, 3)

    first_mean, second_mean = stat_finish(st2, s2_send, s2_recv)
    gi_ref[...] = (
        inv_std * (own[...] - first_mean - normed[...] * second_mean)
    ).astype(BF16)

    for s in (2, -2):
        wait_sibling(1, zm(s))
        project(1, zm(s))
    gg_ref[...] = gain_wait(gx, NX, x, gx_send, gx_recv)[0:1, :]
    for s in (3, -3):
        wait_sibling(1, zm(s))
        project(1, zm(s))
    ring_step(1, 4)
    wait_sibling(1, zm(4))
    project(1, zm(4))

    @pl.loop(0, UNITS // 512)
    def _(i):
        span = pl.ds(pl.multiple_of(i * 512, 512), 512)
        gw_ref[:, span] = gw_ref[:, span] + acc[:, span]

    @pl.when(r != c)
    def _():
        swap.wait_send()

    for ch in range(CH):
        dp_copy(ch).wait_send()

    for ph in range(2):
        @pl.loop(0, 7)
        def _(slot):
            for ch in range(CH):
                remote(
                    act_piece(ph, z, k, ch), act_piece(ph, z, k, ch),
                    ring_send.at[ph, slot, ch], act_recv.at[ph, z, k, ch], sibling,
                ).wait_send()

        @pl.loop(0, 8)
        def _(slot):
            for ch in range(CH):
                sib_copy(ph, z, k, ch, slot).wait_send()

    @pl.loop(0, 7)
    def _(slot):
        hid_copy(0, sibling, hy_send.at[slot]).wait_send()

    @pl.loop(0, 24)
    def _(slot):
        hid_copy(0, sibling, hx_send.at[slot]).wait_send()

    for i in range(4):
        @pl.when(group[i] != x)
        def _():
            rx_copy(group[i], i).wait_send()

    for i in range(1, 4):
        ry_copy(i).wait_send()

    for buf, send, recv in ((st1, s1_send, s1_recv), (st2, s2_send, s2_recv)):
        @pl.loop(1, 16)
        def _(i):
            stat_copy(buf, send, recv, i).wait_send()

    gain_drain(gy, NY, yy, gy_send, gy_recv)
    gain_drain(gx, NX, x, gx_send, gx_recv)


def shards(inputs, gain, w_in, pre_act, grad_act):
    dma = pltpu.SemaphoreType.DMA
    grad_input, grad_w_in, grad_gain = pl.pallas_call(
        kernel,
        out_shape=(
            jax.ShapeDtypeStruct((ROWS, FEAT), BF16),
            jax.ShapeDtypeStruct((FEAT, UNITS), F32),
            jax.ShapeDtypeStruct((1, FEAT), F32),
        ),
        in_specs=[pl.BlockSpec(memory_space=pltpu.VMEM)] * 5,
        out_specs=(pl.BlockSpec(memory_space=pltpu.VMEM),) * 3,
        scratch_shapes=[
            pltpu.VMEM((2, NZ, 2 * ROWS, UNITS), BF16),
            pltpu.VMEM((32, FEAT, ROWS), BF16),
            pltpu.VMEM((FEAT, UNITS), F32),
            pltpu.VMEM((UNITS, FEAT), BF16),
            pltpu.VMEM((NX, 4 * ROWS, FEAT), BF16),
            pltpu.VMEM((NX, 4 * ROWS, FEAT), BF16),
            pltpu.VMEM((ROWS, FEAT), F32),
            pltpu.VMEM((4, ROWS, FEAT), BF16),
            pltpu.VMEM((4, ROWS, FEAT), BF16),
            pltpu.VMEM((ROWS, FEAT), BF16),
            pltpu.VMEM((ROWS, FEAT), F32),
            pltpu.VMEM((16, 8, ROWS), F32),
            pltpu.VMEM((16, 8, ROWS), F32),
            pltpu.VMEM((NY, 8, FEAT), F32),
            pltpu.VMEM((NX, 8, FEAT), F32),
            dma, dma, dma((2, NZ, 2, CH)), dma((2, 7, CH)), dma((2, 8, CH)), dma((CH,)),
            dma((32,)), dma((7,)), dma((24,)), dma((16,)), dma((16,)), dma((16,)), dma((16,)),
            dma((4,)), dma((4,)), dma((4,)), dma((4,)), dma((NY,)), dma((NY,)), dma((NX,)), dma((NX,)),
        ],
        compiler_params=pltpu.CompilerParams(
            collective_id=0, has_side_effects=True, vmem_limit_bytes=56 * 1024 * 1024
        ),
    )(inputs, gain.reshape(1, FEAT), w_in, pre_act, grad_act)
    return grad_input, grad_w_in, grad_gain.reshape(FEAT)


def solution(mesh):
    return jax.shard_map(
        shards,
        mesh=mesh,
        in_specs=(
            P(("dp", "row"), "col"),
            P("row"),
            P("row", "col"),
            P(("dp", "row"), "col"),
            P(("dp", "row"), "col"),
        ),
        out_specs=(P(("dp", "col"), "row"), P("row", "col"), P("row")),
        check_vma=False,
    )
```

time: 541 us -> 140 us (0.26)
  waiting for transfers between devices: 316 us -> 0 us
  blocking collectives: 177 us -> 0 us
  Pallas kernels: 0 us -> 132 us
  matrix products: 15.4 us -> 0 us
  between operations: 13.8 us -> 0.64 us
  other arithmetic: 10.7 us -> 1.26 us
    psum x2 -> x0, waiting for transfers between devices: 187 us -> none  [the longest x1 160 us: spread(): return lax.psum(block, axis)]
    psum x3 -> x0, blocking collectives: 177 us -> none  [the longest x1 87.9 us: shards(): lax.psum(jnp.sum(grad_hidden * own_normed, axis=0), ('dp', 'col'))]
    pallas_call x0 -> x1, Pallas kernels: none -> 132 us  [shards(): pl.pallas_call(kernel, out_shape=(jax.ShapeDtypeStruct((ROWS, FEAT), BF16...]
    all_gather x2 -> x0, waiting for transfers between devices: 96.5 us -> none  [the longest x1 48.3 us: shards(): act_rows = lax.all_gather(act_grad, 'row', axis=0, tiled=True)]
    reduce_scatter x1 -> x0, waiting for transfers between devices: 31.8 us -> none  [shards(): lax.psum_scatter(lax.dot_general(act_rows, w_in, (((1,), (1,)), ((), ()))...]
    dot_general x2 -> x0, matrix products: 15.4 us -> none  [the longest x1 7.93 us: shards(): lax.dot_general(act_rows, w_in, (((1,), (1,)), ((), ())), preferred_eleme...]
  transfers between devices with their start and end apart: 5 -> 0, of which waited for: 5 -> 0; matrix products, arithmetic and copies ran while one was open for 5% -> 0% of each run, Pallas kernels for 0% -> 0%
where the time goes in v1:
time: 140 us
  Pallas kernels  132 us (94%)
  local copies, waits for them, and re-layouts  6.01 us (4%)
    pallas_call x1, Pallas kernels, shards(): pl.pallas_call(kernel, out_shape=(jax.ShapeDtypeStruct((ROWS, FEAT), BF16...  132 us
    unnamed x2, local copies, waits for them, and re-layouts  4.76 us

profile of v1, /device:TPU:1, one launch (start us, length us, event | category | flops | bytes accessed | tf_op | source)
XLA Modules:
  0.0 139.9 jit_solution(1237293417678933501)
XLA Ops:
  0.6 1.2 reshape.12.gain_ref
  1.9 132.0 %shard_map.76 = (bf16[128,384]{1,0:T(8,128)(2,1)}, f32[384,1536]{1,0:T(8,128)}, f32[1,384]{1,0:T(1,128)}) custom-call(bf16[128,384]{1,0:T(8,128)(2,1)} %x_ref.1, f32[1,384]{1,0:T(1,128)} %reshape.12.gain_ref, bf16[384,1536]{1,0:T(8,128)(2,1)} %w_ref.1, bf16[128,1536]{1,0:T(8,128)(2,1)} %pre_ref.1, bf16[128,1536]{1,0:T(8,128)(2,1)} %ga_ref.1), custom_call_target="tpu_custom_call" | custom-call | tf_op jit(solution)/shard_map/pallas_call | solution.py:499
  133.9 1.3 reduce
  135.2 1.5 %copy.10 = bf16[128,384]{1,0:T(8,128)(2,1)} copy(bf16[128,384]{1,0:T(8,128)(2,1)} %get-tuple-element.12) | data formatting | bytes 196608
  136.7 3.2 %copy.11 = f32[384,1536]{1,0:T(8,128)} copy(f32[384,1536]{1,0:T(8,128)} %get-tuple-element.13) | data formatting | bytes 4718592

commit v2 on v1

--- a/solution.py
+++ b/solution.py
@@ -70,6 +70,7 @@
     ym = lambda s: (yy + s + NY) % NY
     xm = lambda s: (x + s + NX) % NX
 
+    gain = gain_ref[...].reshape(1, FEAT)
     barrier = pltpu.get_barrier_semaphore()
 
     def greet(device):
@@ -149,30 +150,25 @@
         start_own(0, ch)
         dp_copy(ch).start()
 
-    def ring_step(ph, s):
-        for ch in range(CH):
-            if s < 4:
-                for sign, slot in ((-1, 0), (1, 1)):
-                    zz = zm(sign * s)
-                    wait_act(ph, zz, k, ch)
-                    if s < 3:
-                        ring_copy(ph, zz, ch, zm(-sign), 2 * s + slot).start()
-                    sib_copy(ph, zz, k, ch, 2 * s - 1 + slot).start()
-                if s == 3:
-                    sign = 2 * k - 1
-                    ring_copy(ph, zm(sign * 3), ch, zm(-sign), 6).start()
-            else:
-                zz = zm(4)
+    def ring_step(ph, s, ch):
+        if s < 4:
+            for sign, slot in ((-1, 0), (1, 1)):
+                zz = zm(sign * s)
                 wait_act(ph, zz, k, ch)
-                sib_copy(ph, zz, k, ch, 7).start()
+                if s < 3:
+                    ring_copy(ph, zz, ch, zm(-sign), 2 * s + slot).start()
+                sib_copy(ph, zz, k, ch, 2 * s - 1 + slot).start()
+            if s == 3:
+                sign = 2 * k - 1
+                ring_copy(ph, zm(sign * 3), ch, zm(-sign), 6).start()
+        else:
+            zz = zm(4)
+            wait_act(ph, zz, k, ch)
+            sib_copy(ph, zz, k, ch, 7).start()
 
     def wait_sibling(ph, zz):
         for ch in range(CH):
             wait_act(ph, zz, 1 - k, ch)
-
-    @pl.when(r != c)
-    def _():
-        swap.wait_recv()
 
     ones = jnp.ones((8, FEAT), F32)
     first_row = lax.broadcasted_iota(jnp.int32, (8, ROWS), 0) == 0
@@ -202,10 +198,6 @@
             total = total + buf[i]
         column = jnp.concatenate([total] * 16, axis=0).T / FEATURES
         return column[:, 0:1], column[:, 1:2]
-
-    values = xin[...].astype(F32)
-    st1[r] = row_pair(values, values * values)
-    stat_start(st1, s1_send, s1_recv)
 
     @pl.loop(0, UNITS // 128)
     def _(i):
@@ -218,15 +210,6 @@
         part[zz // 2, half, :] = jnp.dot(
             act[0, zz], wt[...], preferred_element_type=F32
         ).astype(BF16)
-
-    grad_hidden_part(z)
-
-    row_mean, square_mean = stat_finish(st1, s1_send, s1_recv)
-    variance = square_mean - row_mean * row_mean
-    inv_std = lax.rsqrt(variance + EPSILON)
-    normed[...] = (values - row_mean) * inv_std
-    hidden = normed[...] * gain_ref[...]
-    hid[d * 16 + c] = hidden.T.astype(BF16)
 
     def hid_copy(block, device, send):
         return remote(hid.at[block], hid.at[block], send, h_recv.at[block], device)
@@ -272,10 +255,6 @@
         sign = 2 * k - 1
         hid_copy(hid_block(big, xm(sign)), at_x(xm(-sign)), hx_send.at[3 * slot + 2]).start()
 
-    for sign, slot in ((1, 0), (-1, 1)):
-        hid_copy(hid_block(yy, x), at_y(ym(sign)), hy_send.at[slot]).start()
-    hid_to_x(yy, 0)
-
     def rx_copy(j, i):
         return remote(part.at[j], rx.at[x], rx_send.at[i], rx_recv.at[x], at_x(j))
 
@@ -292,41 +271,7 @@
         (z // 2 + 2) % 4,
     )
 
-    ring_step(0, 1)
-    hid_y_step(1)
-    grad_hidden_part(zm(1))
-    hid_y_step(2)
-    grad_hidden_part(zm(-1))
-    rx_start(group[0], 0)
-    hid_x_step(0)
-
-    ring_step(0, 2)
-    hid_y_step(3)
-    hid_x_step(1)
-    hid_x_step(2)
-    grad_hidden_part(zm(2))
-    hid_y_step(4)
-    grad_hidden_part(zm(-2))
-    rx_start(group[1], 1)
-    hid_x_step(3)
-    hid_x_step(4)
-
-    ring_step(0, 3)
-    for ch in range(CH):
-        wait_act(1, z, k, ch)
-        start_own(1, ch)
-    grad_hidden_part(zm(3))
-    hid_x_step(5)
-    grad_hidden_part(zm(-3))
-    rx_start(group[2], 2)
-    hid_x_step(6)
-    hid_x_step(7)
-
-    ring_step(0, 4)
-    grad_hidden_part(zm(4))
-    rx_start(group[3], 3)
-
-    def project(ph, zz, first=False):
+    def project(ph, zz, first=False, last=False):
         replica = d if ph == 0 else 1 - d
         lhs = jnp.concatenate(
             [hid[replica * 16 + 2 * zz], hid[replica * 16 + 2 * zz + 1]], axis=1
@@ -339,26 +284,10 @@
             out = gw_ref if ph == 0 else acc
             if first:
                 out[:, span] = term
+            elif last:
+                gw_ref[:, span] = gw_ref[:, span] + (acc[:, span] + term)
             else:
                 out[:, span] = out[:, span] + term
-
-    @pl.loop(0, 8)
-    def _(slot):
-        big = (yy + slot) % NY
-        wait_hid(hid_block(big, xm(2)))
-
-    for s in (0, 1, -1, 2):
-        project(0, zm(s), first=s == 0)
-
-    ring_step(1, 1)
-
-    for s in (-2, 3, -3, 4):
-        project(0, zm(s))
-
-    @pl.loop(1, NX)
-    def _(i):
-        other = (x + i) % NX
-        remote(part.at[0], rx.at[other], rx_send.at[0], rx_recv.at[other], sibling).wait_recv()
 
     def x_sum(yq):
         rows = pl.ds(pl.multiple_of(yq * ROWS, ROWS), ROWS)
@@ -371,14 +300,101 @@
         to = (y + i) % 4
         return remote(ty.at[to], ry.at[y], ry_send.at[i], ry_recv.at[y], at(col=x * 4 + to))
 
+    def gain_sum(buf, count, me, send, recv, device_of):
+        @pl.loop(1, count)
+        def _(i):
+            remote(buf.at[me], buf.at[me], send.at[i], recv.at[me], device_of((me + i) % count)).start()
+
+    def gain_wait(buf, count, me, send, recv):
+        @pl.loop(1, count)
+        def _(i):
+            other = (me + i) % count
+            remote(buf.at[other], buf.at[other], send.at[i], recv.at[other], sibling).wait_recv()
+
+        total = buf[0]
+        for i in range(1, count):
+            total = total + buf[i]
+        return total
+
+    def gain_drain(buf, count, me, send, recv):
+        @pl.loop(1, count)
+        def _(i):
+            remote(buf.at[me], buf.at[me], send.at[i], recv.at[me], sibling).wait_send()
+
+    grad_hidden_part(z)
+    ring_step(0, 1, 0)
+
+    @pl.when(r != c)
+    def _():
+        swap.wait_recv()
+
+    values = xin[...].astype(F32)
+    st1[r] = row_pair(values, values * values)
+    stat_start(st1, s1_send, s1_recv)
+    ring_step(0, 1, 1)
+    grad_hidden_part(zm(1))
+    grad_hidden_part(zm(-1))
+    rx_start(group[0], 0)
+
+    row_mean, square_mean = stat_finish(st1, s1_send, s1_recv)
+    variance = square_mean - row_mean * row_mean
+    inv_std = lax.rsqrt(variance + EPSILON)
+    normed[...] = (xin[...].astype(F32) - row_mean) * inv_std
+    hid[d * 16 + c] = (normed[...] * gain).T.astype(BF16)
+    for sign, slot in ((1, 0), (-1, 1)):
+        hid_copy(hid_block(yy, x), at_y(ym(sign)), hy_send.at[slot]).start()
+    hid_to_x(yy, 0)
+
+    ring_step(0, 2, 0)
+    hid_y_step(1)
+    ring_step(0, 2, 1)
+    hid_y_step(2)
+    hid_x_step(0)
+    grad_hidden_part(zm(2))
+    grad_hidden_part(zm(-2))
+    rx_start(group[1], 1)
+    ring_step(0, 3, 0)
+    hid_y_step(3)
+    hid_x_step(1)
+    ring_step(0, 3, 1)
+    for ch in range(CH):
+        wait_act(1, z, k, ch)
+        start_own(1, ch)
+    hid_y_step(4)
+    hid_x_step(2)
+    ring_step(0, 4, 0)
+    hid_x_step(3)
+    ring_step(0, 4, 1)
+    grad_hidden_part(zm(3))
+    grad_hidden_part(zm(-3))
+    rx_start(group[2], 2)
+    grad_hidden_part(zm(4))
+    rx_start(group[3], 3)
+    hid_x_step(4)
+    ring_step(1, 1, 0)
+    hid_x_step(5)
+    hid_x_step(6)
+    hid_x_step(7)
+    ring_step(1, 1, 1)
+
+    @pl.loop(1, NX)
+    def _(i):
+        other = (x + i) % NX
+        remote(part.at[0], rx.at[other], rx_send.at[0], rx_recv.at[other], sibling).wait_recv()
+
     for i in range(1, 4):
         ty[(y + i) % 4] = x_sum((y + i) % 4).astype(BF16)
         ry_copy(i).start()
     own[...] = x_sum(y)
-
-    wait_sibling(1, z)
-    project(1, z, first=True)
-    ring_step(1, 2)
+    ring_step(1, 2, 0)
+
+    @pl.loop(0, 8)
+    def _(slot):
+        big = (yy + slot) % NY
+        wait_hid(hid_block(big, xm(2)))
+
+    for s in (0, 1, -1, 2):
+        project(0, zm(s), first=s == 0)
 
     for i in range(1, 4):
         other = (y + i) % 4
@@ -387,66 +403,45 @@
     for i in range(1, 4):
         grad_hidden = grad_hidden + ry[(y + i) % 4].astype(F32)
 
-    scaled = grad_hidden * gain_ref[...]
+    scaled = grad_hidden * gain
     own_normed = normed[...]
     st2[r] = row_pair(scaled, scaled * own_normed)
     stat_start(st2, s2_send, s2_recv)
     own[...] = scaled
-
-    def gain_sum(buf, count, me, send, recv, device_of):
-        @pl.loop(1, count)
-        def _(i):
-            remote(buf.at[me], buf.at[me], send.at[i], recv.at[me], device_of((me + i) % count)).start()
-
-    def gain_wait(buf, count, me, send, recv):
-        @pl.loop(1, count)
-        def _(i):
-            other = (me + i) % count
-            remote(buf.at[other], buf.at[other], send.at[i], recv.at[other], sibling).wait_recv()
-
-        total = buf[0]
-        for i in range(1, count):
-            total = total + buf[i]
-        return total
-
-    def gain_drain(buf, count, me, send, recv):
-        @pl.loop(1, count)
-        def _(i):
-            remote(buf.at[me], buf.at[me], send.at[i], recv.at[me], sibling).wait_send()
-
     gy[yy] = jnp.broadcast_to(
         jnp.sum(grad_hidden * own_normed, axis=0, keepdims=True), (8, FEAT)
     )
     gain_sum(gy, NY, yy, gy_send, gy_recv, at_y)
-
-    for s in (1, -1):
-        wait_sibling(1, zm(s))
-        project(1, zm(s))
-
+    ring_step(1, 2, 1)
+
+    for s in (-2, 3, -3, 4):
+        project(0, zm(s))
+
+    wait_sibling(1, z)
+    project(1, z, first=True)
+    ring_step(1, 3, 0)
     gx[x] = gain_wait(gy, NY, yy, gy_send, gy_recv)
     gain_sum(gx, NX, x, gx_send, gx_recv, at_x)
-    ring_step(1, 3)
 
     first_mean, second_mean = stat_finish(st2, s2_send, s2_recv)
     gi_ref[...] = (
         inv_std * (own[...] - first_mean - normed[...] * second_mean)
     ).astype(BF16)
-
+    for s in (1, -1):
+        wait_sibling(1, zm(s))
+        project(1, zm(s))
+    ring_step(1, 3, 1)
     for s in (2, -2):
         wait_sibling(1, zm(s))
         project(1, zm(s))
-    gg_ref[...] = gain_wait(gx, NX, x, gx_send, gx_recv)[0:1, :]
+    gg_ref[...] = gain_wait(gx, NX, x, gx_send, gx_recv)[0]
+    ring_step(1, 4, 0)
     for s in (3, -3):
         wait_sibling(1, zm(s))
         project(1, zm(s))
-    ring_step(1, 4)
+    ring_step(1, 4, 1)
     wait_sibling(1, zm(4))
-    project(1, zm(4))
-
-    @pl.loop(0, UNITS // 512)
-    def _(i):
-        span = pl.ds(pl.multiple_of(i * 512, 512), 512)
-        gw_ref[:, span] = gw_ref[:, span] + acc[:, span]
+    project(1, zm(4), last=True)
 
     @pl.when(r != c)
     def _():
@@ -500,8 +495,8 @@
         kernel,
         out_shape=(
             jax.ShapeDtypeStruct((ROWS, FEAT), BF16),
-            jax.ShapeDtypeStruct((FEAT, UNITS), F32),
-            jax.ShapeDtypeStruct((1, FEAT), F32),
+            pltpu.VMEM((FEAT, UNITS), F32),
+            jax.ShapeDtypeStruct((FEAT,), F32),
         ),
         in_specs=[pl.BlockSpec(memory_space=pltpu.VMEM)] * 5,
         out_specs=(pl.BlockSpec(memory_space=pltpu.VMEM),) * 3,
@@ -526,10 +521,10 @@
             dma((4,)), dma((4,)), dma((4,)), dma((4,)), dma((NY,)), dma((NY,)), dma((NX,)), dma((NX,)),
         ],
         compiler_params=pltpu.CompilerParams(
-            collective_id=0, has_side_effects=True, vmem_limit_bytes=56 * 1024 * 1024
+            collective_id=0, has_side_effects=True, vmem_limit_bytes=40 * 1024 * 1024
         ),
-    )(inputs, gain.reshape(1, FEAT), w_in, pre_act, grad_act)
-    return grad_input, grad_w_in, grad_gain.reshape(FEAT)
+    )(inputs, gain, w_in, pre_act, grad_act)
+    return grad_input, grad_w_in, grad_gain
 
 
 def solution(mesh):

time: 140 us -> 129 us (0.921)
  Pallas kernels: 132 us -> 120 us
  local copies, waits for them, and re-layouts: 6.01 us -> 7.45 us
    pallas_call x1, Pallas kernels: 132 us -> 120 us  [shards(): pl.pallas_call(kernel, out_shape=(jax.ShapeDtypeStruct((ROWS, FEAT), BF16...]
    unnamed x2 -> x13, local copies, waits for them, and re-layouts: 4.76 us -> 7.45 us
where the time goes in v2:
time: 129 us; the launch traced here: 128 us
  Pallas kernels  120 us (93%)
  local copies, waits for them, and re-layouts  7.45 us (6%)
    pallas_call x1, Pallas kernels, shards(): pl.pallas_call(kernel, out_shape=(jax.ShapeDtypeStruct((ROWS, FEAT), BF16...  120 us
    unnamed x13, local copies, waits for them, and re-layouts  7.45 us

profile of v2, /device:TPU:1, one launch (start us, length us, event | category | flops | bytes accessed | tf_op | source)
XLA Modules:
  0.0 128.5 jit_solution(4910193276784482824)
XLA Ops:
  0.6 0.0 copy-start
  0.6 1.3 copy-done
  1.9 0.0 copy-start.1
  1.9 1.0 copy-done.1
  2.9 0.0 copy-start.2
  2.9 1.0 copy-done.2
  3.9 0.0 copy-start.3
  3.9 0.9 copy-done.3
  4.8 0.0 copy-start.4
  4.8 0.7 copy-done.4
  5.5 120.4 %shard_map.76 = (bf16[128,384]{1,0:T(8,128)(2,1)S(1)}, f32[384,1536]{1,0:T(8,128)S(1)}, f32[384]{0:T(512)S(1)}) custom-call(bf16[128,384]{1,0:T(8,128)(2,1)S(1)} %copy-done.3, f32[384]{0:T(512)S(1)} %copy-done.4, bf16[384,1536]{1,0:T(8,128)(2,1)S(1)} %copy-done, bf16[128,1536]{1,0:T(8,128)(2,1)S(1)} %copy-done.1, bf16[128,1536]{1,0:T(8,128)(2,1)S(1)} %copy-done.2), custom_call_target="tpu_custom_call" | custom-call | tf_op jit(solution)/shard_map/pallas_call | solution.py:494
  125.8 1.4 %copy.11 = f32[384,1536]{1,0:T(8,128)} copy(f32[384,1536]{1,0:T(8,128)S(1)} %get-tuple-element.4) | data formatting | bytes 4718592
  127.2 0.6 copy.12
  127.9 0.6 copy.13
Async XLA Ops:
  0.6 1.3 copy-start
  1.9 1.0 copy-start.1
  2.9 1.0 copy-start.2
  3.9 0.9 copy-start.3
  4.8 0.7 copy-start.4

commit v3 on v2

--- a/solution.py
+++ b/solution.py
@@ -31,10 +31,11 @@
 
 
 def kernel(
-    x_ref, gain_ref, w_ref, pre_ref, ga_ref,
+    x_in, gain_in, w_in, pre_in, ga_in,
     gi_ref, gw_ref, gg_ref,
-    act, hid, acc, wt, part, rx, own, ty, ry, xin, normed, st1, st2, gy, gx,
-    xt_send, xt_recv, act_recv, ring_send, sib_send, dp_send,
+    x_ref, gain_ref, w_ref, pre_ref, ga_ref, load,
+    act, hid, acc, wt, part, rx, own, ty, ry, xin, normed, st1, st2, stot, stin, gy, gx,
+    xt_send, xt_recv, sin_send, sin_recv, act_recv, ring_send, sib_send, dp_send,
     h_recv, hy_send, hx_send, s1_send, s1_recv, s2_send, s2_recv,
     rx_send, rx_recv, ry_send, ry_recv, gy_send, gy_recv, gx_send, gx_recv,
 ):
@@ -70,7 +71,15 @@
     ym = lambda s: (yy + s + NY) % NY
     xm = lambda s: (x + s + NX) % NX
 
-    gain = gain_ref[...].reshape(1, FEAT)
+    loads = [
+        pltpu.make_async_copy(src, dst, load.at[i])
+        for i, (src, dst) in enumerate(
+            ((pre_in, pre_ref), (ga_in, ga_ref), (x_in, x_ref), (gain_in, gain_ref), (w_in, w_ref))
+        )
+    ]
+    for copy in loads:
+        copy.start()
+
     barrier = pltpu.get_barrier_semaphore()
 
     def greet(device):
@@ -80,13 +89,13 @@
     def _(i):
         greet(at(row=(r + i) % 16))
 
-    @pl.loop(1, NY)
+    @pl.loop(1, 16)
     def _(i):
-        greet(at_y((yy + i) % NY))
-
-    @pl.loop(1, NX)
+        greet(at(col=(c + i) % 16))
+
+    @pl.loop(0, 4)
     def _(i):
-        greet(at_x((x + i) % NX))
+        greet(at(dp=1 - d, col=x * 4 + i))
 
     @pl.when(r != c)
     def _():
@@ -94,11 +103,15 @@
 
     @pl.when(r != c)
     def _():
-        pl.semaphore_wait(barrier, 15 + NY - 1 + NX - 1 + 1)
+        pl.semaphore_wait(barrier, 15 + 15 + 4 + 1)
 
     @pl.when(r == c)
     def _():
-        pl.semaphore_wait(barrier, 15 + NY - 1 + NX - 1)
+        pl.semaphore_wait(barrier, 15 + 15 + 4)
+
+    for copy in loads:
+        copy.wait()
+    gain = gain_ref[...].reshape(1, FEAT)
 
     swap = remote(x_ref, xin, xt_send, xt_recv, at(row=c, col=r))
 
@@ -148,7 +161,8 @@
             act[0, z, there, :] = (ga_ref[here, :].astype(F32) * slopes).astype(BF16)
 
         start_own(0, ch)
-        dp_copy(ch).start()
+        if ch == 0:
+            dp_copy(ch).start()
 
     def ring_step(ph, s, ch):
         if s < 4:
@@ -179,37 +193,57 @@
         sum_b = lax.dot_general(ones, b, dims, precision=HIGH, preferred_element_type=F32)
         return jnp.where(first_row, sum_a, sum_b)
 
-    def stat_copy(buf, send, recv, i):
-        return remote(buf.at[r], buf.at[r], send.at[i], recv.at[r], at(row=(r + i) % 16))
-
-    def stat_start(buf, send, recv):
+    def stat_peer(axis, i):
+        return at(row=(r + i) % 16) if axis == "row" else at(col=(c + i) % 16)
+
+    def stat_copy(buf, send, recv, axis, i):
+        me = r if axis == "row" else c
+        return remote(buf.at[me], buf.at[me], send.at[i], recv.at[me], stat_peer(axis, i))
+
+    def stat_start(buf, send, recv, axis):
         @pl.loop(1, 16)
         def _(i):
-            stat_copy(buf, send, recv, i).start()
-
-    def stat_finish(buf, send, recv):
+            stat_copy(buf, send, recv, axis, i).start()
+
+    def stat_finish(buf, send, recv, axis):
         @pl.loop(1, 16)
         def _(i):
-            other = (r + i) % 16
+            other = ((r if axis == "row" else c) + i) % 16
             remote(buf.at[other], buf.at[other], send.at[i], recv.at[other], sibling).wait_recv()
 
         total = buf[0]
         for i in range(1, 16):
             total = total + buf[i]
+        return total
+
+    def columns_of(total):
         column = jnp.concatenate([total] * 16, axis=0).T / FEATURES
         return column[:, 0:1], column[:, 1:2]
+
+    values = x_ref[...].astype(F32)
+    st1[c] = row_pair(values, values * values)
+    stat_start(st1, s1_send, s1_recv, "col")
+    total_copy = remote(stot, stin, sin_send, sin_recv, at(row=c, col=r))
 
     @pl.loop(0, UNITS // 128)
     def _(i):
         span = pl.ds(pl.multiple_of(i * 128, 128), 128)
         wt[span, :] = w_ref[:, span].T
 
-    def grad_hidden_part(zz):
+    def rx_copy(zz, i):
+        half = pl.ds(pl.multiple_of((zz % 2) * 256, 256), 256)
+        return remote(
+            part.at[zz], rx.at[x, half], rx_send.at[i], rx_recv.at[x, zz % 2], at_x(zz // 2)
+        )
+
+    def grad_hidden_part(s, i):
+        zz = zm(s)
         wait_sibling(0, zz)
-        half = pl.ds(pl.multiple_of((zz % 2) * 256, 256), 256)
-        part[zz // 2, half, :] = jnp.dot(
-            act[0, zz], wt[...], preferred_element_type=F32
-        ).astype(BF16)
+        part[zz] = jnp.dot(act[0, zz], wt[...], preferred_element_type=F32).astype(BF16)
+
+        @pl.when(zz // 2 != x)
+        def _():
+            rx_copy(zz, i).start()
 
     def hid_copy(block, device, send):
         return remote(hid.at[block], hid.at[block], send, h_recv.at[block], device)
@@ -217,59 +251,49 @@
     def hid_block(big, xx):
         return (big // 4) * 16 + xx * 4 + big % 4
 
-    def hid_to_x(big, slot):
+    def hid_to_x(big):
         block = hid_block(big, x)
-        hid_copy(block, at_x(xm(1)), hx_send.at[3 * slot]).start()
-        hid_copy(block, at_x(xm(-1)), hx_send.at[3 * slot + 1]).start()
+        hid_copy(block, at_x(xm(1)), hx_send.at[3 * big]).start()
+        hid_copy(block, at_x(xm(-1)), hx_send.at[3 * big + 1]).start()
 
     def wait_hid(block):
         hid_copy(block, sibling, hx_send.at[0]).wait_recv()
+
+    def hid_arrived(big):
+        wait_hid(hid_block(big, x))
+
+        @pl.when(big // 4 == d)
+        def _():
+            hid_to_x(big)
 
     def hid_y_step(s):
         if s < 4:
             for sign, slot in ((-1, 0), (1, 1)):
                 big = ym(sign * s)
-                wait_hid(hid_block(big, x))
+                hid_arrived(big)
                 if s < 3:
                     hid_copy(hid_block(big, x), at_y(ym(-sign)), hy_send.at[2 * s + slot]).start()
-                hid_to_x(big, 2 * s - 1 + slot)
             if s == 3:
                 sign = 2 * k - 1
                 hid_copy(hid_block(ym(3 * sign), x), at_y(ym(-sign)), hy_send.at[6]).start()
         else:
-            big = ym(4)
-            wait_hid(hid_block(big, x))
-            hid_to_x(big, 7)
-
-    def y_of(slot):
-        if slot == 0:
-            return yy
-        if slot == 7:
-            return ym(4)
-        return ym((1, -1)[slot % 2] * ((slot + 1) // 2))
-
-    def hid_x_step(slot):
-        big = y_of(slot)
+            hid_arrived(ym(4))
+
+    def hid_others():
+        for i in range(4):
+            hid_to_x((1 - d) * 4 + (y + i) % 4)
+
+    def hid_x_step(ph, i):
+        big = (d if ph == 0 else 1 - d) * 4 + (y + i) % 4
         wait_hid(hid_block(big, xm(1)))
         wait_hid(hid_block(big, xm(-1)))
         sign = 2 * k - 1
-        hid_copy(hid_block(big, xm(sign)), at_x(xm(-sign)), hx_send.at[3 * slot + 2]).start()
-
-    def rx_copy(j, i):
-        return remote(part.at[j], rx.at[x], rx_send.at[i], rx_recv.at[x], at_x(j))
-
-    def rx_start(j, i):
-        @pl.when(j != x)
-        def _():
-            rx_copy(j, i).start()
-
-    even = 1 - z % 2
-    group = (
-        z // 2,
-        (z // 2 + 4 + 1 - 2 * even) % 4,
-        (z // 2 + 4 - 1 + 2 * even) % 4,
-        (z // 2 + 2) % 4,
-    )
+        hid_copy(hid_block(big, xm(sign)), at_x(xm(-sign)), hx_send.at[3 * big + 2]).start()
+
+    def hid_ready(ph):
+        @pl.loop(0, 4)
+        def _(i):
+            wait_hid(hid_block((d if ph == 0 else 1 - d) * 4 + i, xm(2)))
 
     def project(ph, zz, first=False, last=False):
         replica = d if ph == 0 else 1 - d
@@ -291,7 +315,8 @@
 
     def x_sum(yq):
         rows = pl.ds(pl.multiple_of(yq * ROWS, ROWS), ROWS)
-        total = part[x, rows, :].astype(F32)
+        inner = pl.ds(pl.multiple_of((yq % 2) * ROWS, ROWS), ROWS)
+        total = part[2 * x + yq // 2, inner, :].astype(F32)
         for i in range(1, NX):
             total = total + rx[xm(i), rows, :].astype(F32)
         return total
@@ -321,80 +346,89 @@
         def _(i):
             remote(buf.at[me], buf.at[me], send.at[i], recv.at[me], sibling).wait_send()
 
-    grad_hidden_part(z)
+    grad_hidden_part(0, 0)
+    stot[...] = stat_finish(st1, s1_send, s1_recv, "col")
+
+    @pl.when(r != c)
+    def _():
+        total_copy.start()
+
+    @pl.when(r == c)
+    def _():
+        stin[...] = stot[...]
+
     ring_step(0, 1, 0)
+    ring_step(0, 1, 1)
 
     @pl.when(r != c)
     def _():
         swap.wait_recv()
-
-    values = xin[...].astype(F32)
-    st1[r] = row_pair(values, values * values)
-    stat_start(st1, s1_send, s1_recv)
-    ring_step(0, 1, 1)
-    grad_hidden_part(zm(1))
-    grad_hidden_part(zm(-1))
-    rx_start(group[0], 0)
-
-    row_mean, square_mean = stat_finish(st1, s1_send, s1_recv)
+        total_copy.wait_recv()
+
+    row_mean, square_mean = columns_of(stin[...])
     variance = square_mean - row_mean * row_mean
     inv_std = lax.rsqrt(variance + EPSILON)
     normed[...] = (xin[...].astype(F32) - row_mean) * inv_std
     hid[d * 16 + c] = (normed[...] * gain).T.astype(BF16)
     for sign, slot in ((1, 0), (-1, 1)):
         hid_copy(hid_block(yy, x), at_y(ym(sign)), hy_send.at[slot]).start()
-    hid_to_x(yy, 0)
-
+    hid_to_x(yy)
+    dp_copy(1).start()
+
+    grad_hidden_part(1, 1)
+    grad_hidden_part(-1, 2)
     ring_step(0, 2, 0)
     hid_y_step(1)
+    hid_x_step(0, 0)
     ring_step(0, 2, 1)
+    grad_hidden_part(2, 3)
+    grad_hidden_part(-2, 4)
     hid_y_step(2)
-    hid_x_step(0)
-    grad_hidden_part(zm(2))
-    grad_hidden_part(zm(-2))
-    rx_start(group[1], 1)
     ring_step(0, 3, 0)
+    wait_act(1, z, k, 0)
+    start_own(1, 0)
     hid_y_step(3)
-    hid_x_step(1)
     ring_step(0, 3, 1)
-    for ch in range(CH):
-        wait_act(1, z, k, ch)
-        start_own(1, ch)
+    wait_act(1, z, k, 1)
+    start_own(1, 1)
+    grad_hidden_part(3, 5)
+    grad_hidden_part(-3, 6)
+    ring_step(0, 4, 0)
     hid_y_step(4)
-    hid_x_step(2)
-    ring_step(0, 4, 0)
-    hid_x_step(3)
+    hid_x_step(0, 1)
+    hid_x_step(0, 2)
+    hid_x_step(0, 3)
+    ring_step(1, 1, 0)
     ring_step(0, 4, 1)
-    grad_hidden_part(zm(3))
-    grad_hidden_part(zm(-3))
-    rx_start(group[2], 2)
-    grad_hidden_part(zm(4))
-    rx_start(group[3], 3)
-    hid_x_step(4)
-    ring_step(1, 1, 0)
-    hid_x_step(5)
-    hid_x_step(6)
-    hid_x_step(7)
+    grad_hidden_part(4, 7)
+    hid_others()
+    hid_ready(0)
     ring_step(1, 1, 1)
-
-    @pl.loop(1, NX)
-    def _(i):
-        other = (x + i) % NX
-        remote(part.at[0], rx.at[other], rx_send.at[0], rx_recv.at[other], sibling).wait_recv()
+    for s in (0, 1, -1, 2, -2, 3):
+        project(0, zm(s), first=s == 0)
+    ring_step(1, 2, 0)
+
+    for half in range(2):
+        @pl.loop(1, NX)
+        def _(i):
+            other = (x + i) % NX
+            rows = pl.ds(half * 256, 256)
+            remote(
+                part.at[0], rx.at[other, rows], rx_send.at[0], rx_recv.at[other, half], sibling
+            ).wait_recv()
 
     for i in range(1, 4):
         ty[(y + i) % 4] = x_sum((y + i) % 4).astype(BF16)
         ry_copy(i).start()
     own[...] = x_sum(y)
-    ring_step(1, 2, 0)
-
-    @pl.loop(0, 8)
-    def _(slot):
-        big = (yy + slot) % NY
-        wait_hid(hid_block(big, xm(2)))
-
-    for s in (0, 1, -1, 2):
-        project(0, zm(s), first=s == 0)
+    hid_x_step(1, 0)
+    hid_x_step(1, 1)
+    ring_step(1, 2, 1)
+    hid_x_step(1, 2)
+    hid_x_step(1, 3)
+    for s in (-3, 4):
+        project(0, zm(s))
+    ring_step(1, 3, 0)
 
     for i in range(1, 4):
         other = (y + i) % 4
@@ -406,46 +440,41 @@
     scaled = grad_hidden * gain
     own_normed = normed[...]
     st2[r] = row_pair(scaled, scaled * own_normed)
-    stat_start(st2, s2_send, s2_recv)
+    stat_start(st2, s2_send, s2_recv, "row")
     own[...] = scaled
     gy[yy] = jnp.broadcast_to(
         jnp.sum(grad_hidden * own_normed, axis=0, keepdims=True), (8, FEAT)
     )
     gain_sum(gy, NY, yy, gy_send, gy_recv, at_y)
-    ring_step(1, 2, 1)
-
-    for s in (-2, 3, -3, 4):
-        project(0, zm(s))
-
+    ring_step(1, 3, 1)
+    hid_ready(1)
     wait_sibling(1, z)
     project(1, z, first=True)
-    ring_step(1, 3, 0)
+    for s in (1, -1):
+        wait_sibling(1, zm(s))
+        project(1, zm(s))
+    ring_step(1, 4, 0)
     gx[x] = gain_wait(gy, NY, yy, gy_send, gy_recv)
     gain_sum(gx, NX, x, gx_send, gx_recv, at_x)
-
-    first_mean, second_mean = stat_finish(st2, s2_send, s2_recv)
+    for s in (2, -2):
+        wait_sibling(1, zm(s))
+        project(1, zm(s))
+    first_mean, second_mean = columns_of(stat_finish(st2, s2_send, s2_recv, "row"))
     gi_ref[...] = (
         inv_std * (own[...] - first_mean - normed[...] * second_mean)
     ).astype(BF16)
-    for s in (1, -1):
-        wait_sibling(1, zm(s))
-        project(1, zm(s))
-    ring_step(1, 3, 1)
-    for s in (2, -2):
-        wait_sibling(1, zm(s))
-        project(1, zm(s))
-    gg_ref[...] = gain_wait(gx, NX, x, gx_send, gx_recv)[0]
-    ring_step(1, 4, 0)
+    ring_step(1, 4, 1)
     for s in (3, -3):
         wait_sibling(1, zm(s))
         project(1, zm(s))
-    ring_step(1, 4, 1)
     wait_sibling(1, zm(4))
     project(1, zm(4), last=True)
+    gg_ref[...] = gain_wait(gx, NX, x, gx_send, gx_recv)[0]
 
     @pl.when(r != c)
     def _():
         swap.wait_send()
+        total_copy.wait_send()
 
     for ch in range(CH):
         dp_copy(ch).wait_send()
@@ -472,18 +501,18 @@
     def _(slot):
         hid_copy(0, sibling, hx_send.at[slot]).wait_send()
 
-    for i in range(4):
-        @pl.when(group[i] != x)
+    for i, step in enumerate((0, 1, -1, 2, -2, 3, -3, 4)):
+        @pl.when(zm(step) // 2 != x)
         def _():
-            rx_copy(group[i], i).wait_send()
+            rx_copy(zm(step), i).wait_send()
 
     for i in range(1, 4):
         ry_copy(i).wait_send()
 
-    for buf, send, recv in ((st1, s1_send, s1_recv), (st2, s2_send, s2_recv)):
+    for buf, send, recv, axis in ((st1, s1_send, s1_recv, "col"), (st2, s2_send, s2_recv, "row")):
         @pl.loop(1, 16)
         def _(i):
-            stat_copy(buf, send, recv, i).wait_send()
+            stat_copy(buf, send, recv, axis, i).wait_send()
 
     gain_drain(gy, NY, yy, gy_send, gy_recv)
     gain_drain(gx, NX, x, gx_send, gx_recv)
@@ -498,14 +527,20 @@
             pltpu.VMEM((FEAT, UNITS), F32),
             jax.ShapeDtypeStruct((FEAT,), F32),
         ),
-        in_specs=[pl.BlockSpec(memory_space=pltpu.VMEM)] * 5,
+        in_specs=[pl.BlockSpec(memory_space=pltpu.HBM)] * 5,
         out_specs=(pl.BlockSpec(memory_space=pltpu.VMEM),) * 3,
         scratch_shapes=[
+            pltpu.VMEM((ROWS, FEAT), BF16),
+            pltpu.VMEM((FEAT,), F32),
+            pltpu.VMEM((FEAT, UNITS), BF16),
+            pltpu.VMEM((ROWS, UNITS), BF16),
+            pltpu.VMEM((ROWS, UNITS), BF16),
+            dma((5,)),
             pltpu.VMEM((2, NZ, 2 * ROWS, UNITS), BF16),
             pltpu.VMEM((32, FEAT, ROWS), BF16),
             pltpu.VMEM((FEAT, UNITS), F32),
             pltpu.VMEM((UNITS, FEAT), BF16),
-            pltpu.VMEM((NX, 4 * ROWS, FEAT), BF16),
+            pltpu.VMEM((NZ, 2 * ROWS, FEAT), BF16),
             pltpu.VMEM((NX, 4 * ROWS, FEAT), BF16),
             pltpu.VMEM((ROWS, FEAT), F32),
             pltpu.VMEM((4, ROWS, FEAT), BF16),
@@ -514,16 +549,23 @@
             pltpu.VMEM((ROWS, FEAT), F32),
             pltpu.VMEM((16, 8, ROWS), F32),
             pltpu.VMEM((16, 8, ROWS), F32),
+            pltpu.VMEM((8, ROWS), F32),
+            pltpu.VMEM((8, ROWS), F32),
             pltpu.VMEM((NY, 8, FEAT), F32),
             pltpu.VMEM((NX, 8, FEAT), F32),
-            dma, dma, dma((2, NZ, 2, CH)), dma((2, 7, CH)), dma((2, 8, CH)), dma((CH,)),
+            dma, dma, dma, dma, dma((2, NZ, 2, CH)), dma((2, 7, CH)), dma((2, 8, CH)), dma((CH,)),
             dma((32,)), dma((7,)), dma((24,)), dma((16,)), dma((16,)), dma((16,)), dma((16,)),
-            dma((4,)), dma((4,)), dma((4,)), dma((4,)), dma((NY,)), dma((NY,)), dma((NX,)), dma((NX,)),
+            dma((8,)), dma((NX, 2)), dma((4,)), dma((4,)), dma((NY,)), dma((NY,)), dma((NX,)), dma((NX,)),
         ],
         compiler_params=pltpu.CompilerParams(
             collective_id=0, has_side_effects=True, vmem_limit_bytes=40 * 1024 * 1024
         ),
-    )(inputs, gain, w_in, pre_act, grad_act)
+    )(
+        *(
+            pltpu.with_memory_space_constraint(a, pltpu.HBM)
+            for a in (inputs, gain, w_in, pre_act, grad_act)
+        )
+    )
     return grad_input, grad_w_in, grad_gain
 
 

time: 129 us -> 110 us (0.85)
  the two profiles are of different devices: /device:TPU:1 before, /device:TPU:20 now
where the time goes in v3:
time: 110 us; the launch traced here: 109 us
  Pallas kernels  106 us (96%)
  local copies, waits for them, and re-layouts  2.63 us (2%)
    pallas_call x1, Pallas kernels, shards(): pl.pallas_call(kernel, out_shape=(jax.ShapeDtypeStruct((ROWS, FEAT), BF16...  106 us
    unnamed x3, local copies, waits for them, and re-layouts  2.63 us

profile of v3, /device:TPU:20, one launch (start us, length us, event | category | flops | bytes accessed | tf_op | source)
XLA Modules:
  0.0 109.5 jit_solution(15792110201962365121)
XLA Ops:
  0.6 106.2 %shard_map.76 = (bf16[128,384]{1,0:T(8,128)(2,1)S(1)}, f32[384,1536]{1,0:T(8,128)S(1)}, f32[384]{0:T(512)S(1)}) custom-call(bf16[128,384]{1,0:T(8,128)(2,1)} %x_in.1, f32[384]{0:T(512)} %gain_in.1, bf16[384,1536]{1,0:T(8,128)(2,1)} %w_in.1, bf16[128,1536]{1,0:T(8,128)(2,1)} %pre_in.1, bf16[128,1536]{1,0:T(8,128)(2,1)} %ga_in.1), custom_call_target="tpu_custom_call" | custom-call | tf_op jit(solution)/shard_map/pallas_call | solution.py:523
  106.8 1.4 %copy.11 = f32[384,1536]{1,0:T(8,128)} copy(f32[384,1536]{1,0:T(8,128)S(1)} %get-tuple-element.4) | data formatting | bytes 4718592
  108.3 0.6 copy.12
  108.9 0.6 copy.13

commit v4 on v3

--- a/solution.py
+++ b/solution.py
@@ -101,17 +101,27 @@
     def _():
         greet(at(row=c, col=r))
 
-    @pl.when(r != c)
-    def _():
-        pl.semaphore_wait(barrier, 15 + 15 + 4 + 1)
-
-    @pl.when(r == c)
-    def _():
-        pl.semaphore_wait(barrier, 15 + 15 + 4)
-
-    for copy in loads:
+    loads[0].wait()
+    loads[1].wait()
+
+    @pl.loop(0, ROWS // 16)
+    def _(i):
+        here = pl.ds(pl.multiple_of(i * 16, 16), 16)
+        there = pl.ds(pl.multiple_of(k * ROWS + i * 16, 16), 16)
+        slopes = gelu_slope(pre_ref[here, :].astype(F32))
+        act[0, z, there, :] = (ga_ref[here, :].astype(F32) * slopes).astype(BF16)
+
+    for copy in loads[2:]:
         copy.wait()
     gain = gain_ref[...].reshape(1, FEAT)
+
+    @pl.when(r != c)
+    def _():
+        pl.semaphore_wait(barrier, 15 + 15 + 4 + 1)
+
+    @pl.when(r == c)
+    def _():
+        pl.semaphore_wait(barrier, 15 + 15 + 4)
 
     swap = remote(x_ref, xin, xt_send, xt_recv, at(row=c, col=r))
 
@@ -153,13 +163,6 @@
         sib_copy(ph, z, k, ch, 0).start()
 
     for ch in range(CH):
-        @pl.loop(0, CROWS // 16)
-        def _(i):
-            here = pl.ds(pl.multiple_of(ch * CROWS + i * 16, 16), 16)
-            there = pl.ds(pl.multiple_of(k * ROWS + ch * CROWS + i * 16, 16), 16)
-            slopes = gelu_slope(pre_ref[here, :].astype(F32))
-            act[0, z, there, :] = (ga_ref[here, :].astype(F32) * slopes).astype(BF16)
-
         start_own(0, ch)
         if ch == 0:
             dp_copy(ch).start()
@@ -191,7 +194,7 @@
         dims = (((1,), (1,)), ((), ()))
         sum_a = lax.dot_general(ones, a, dims, precision=HIGH, preferred_element_type=F32)
         sum_b = lax.dot_general(ones, b, dims, precision=HIGH, preferred_element_type=F32)
-        return jnp.where(first_row, sum_a, sum_b)
+        return jnp.where(first_row, sum_a, sum_b)[0:2]
 
     def stat_peer(axis, i):
         return at(row=(r + i) % 16) if axis == "row" else at(col=(c + i) % 16)
@@ -217,7 +220,7 @@
         return total
 
     def columns_of(total):
-        column = jnp.concatenate([total] * 16, axis=0).T / FEATURES
+        column = jnp.concatenate([total, jnp.zeros((ROWS - 2, ROWS), F32)], axis=0).T / FEATURES
         return column[:, 0:1], column[:, 1:2]
 
     values = x_ref[...].astype(F32)
@@ -385,12 +388,11 @@
     grad_hidden_part(-2, 4)
     hid_y_step(2)
     ring_step(0, 3, 0)
-    wait_act(1, z, k, 0)
-    start_own(1, 0)
     hid_y_step(3)
     ring_step(0, 3, 1)
-    wait_act(1, z, k, 1)
-    start_own(1, 1)
+    for ch in range(CH):
+        wait_act(1, z, k, ch)
+        start_own(1, ch)
     grad_hidden_part(3, 5)
     grad_hidden_part(-3, 6)
     ring_step(0, 4, 0)
@@ -439,13 +441,11 @@
 
     scaled = grad_hidden * gain
     own_normed = normed[...]
+    gy[yy] = jnp.sum(grad_hidden * own_normed, axis=0, keepdims=True)
+    gain_sum(gy, NY, yy, gy_send, gy_recv, at_y)
     st2[r] = row_pair(scaled, scaled * own_normed)
     stat_start(st2, s2_send, s2_recv, "row")
     own[...] = scaled
-    gy[yy] = jnp.broadcast_to(
-        jnp.sum(grad_hidden * own_normed, axis=0, keepdims=True), (8, FEAT)
-    )
-    gain_sum(gy, NY, yy, gy_send, gy_recv, at_y)
     ring_step(1, 3, 1)
     hid_ready(1)
     wait_sibling(1, z)
@@ -547,12 +547,12 @@
             pltpu.VMEM((4, ROWS, FEAT), BF16),
             pltpu.VMEM((ROWS, FEAT), BF16),
             pltpu.VMEM((ROWS, FEAT), F32),
-            pltpu.VMEM((16, 8, ROWS), F32),
-            pltpu.VMEM((16, 8, ROWS), F32),
-            pltpu.VMEM((8, ROWS), F32),
-            pltpu.VMEM((8, ROWS), F32),
-            pltpu.VMEM((NY, 8, FEAT), F32),
-            pltpu.VMEM((NX, 8, FEAT), F32),
+            pltpu.VMEM((16, 2, ROWS), F32),
+            pltpu.VMEM((16, 2, ROWS), F32),
+            pltpu.VMEM((2, ROWS), F32),
+            pltpu.VMEM((2, ROWS), F32),
+            pltpu.VMEM((NY, 1, FEAT), F32),
+            pltpu.VMEM((NX, 1, FEAT), F32),
             dma, dma, dma, dma, dma((2, NZ, 2, CH)), dma((2, 7, CH)), dma((2, 8, CH)), dma((CH,)),
             dma((32,)), dma((7,)), dma((24,)), dma((16,)), dma((16,)), dma((16,)), dma((16,)),
             dma((8,)), dma((NX, 2)), dma((4,)), dma((4,)), dma((NY,)), dma((NY,)), dma((NX,)), dma((NX,)),

time: 110 us -> 107 us (0.973)
  the two profiles are of different devices: /device:TPU:20 before, /device:TPU:1 now
where the time goes in v4:
time: 107 us; the launch traced here: 106 us
  Pallas kernels  102 us (95%)
  local copies, waits for them, and re-layouts  2.63 us (2%)
    pallas_call x1, Pallas kernels, shards(): pl.pallas_call(kernel, out_shape=(jax.ShapeDtypeStruct((ROWS, FEAT), BF16...  102 us
    unnamed x3, local copies, waits for them, and re-layouts  2.63 us

profile of v4, /device:TPU:1, one launch (start us, length us, event | category | flops | bytes accessed | tf_op | source)
XLA Modules:
  0.0 105.5 jit_solution(1012490474967955151)
XLA Ops:
  0.6 102.2 %shard_map.76 = (bf16[128,384]{1,0:T(8,128)(2,1)S(1)}, f32[384,1536]{1,0:T(8,128)S(1)}, f32[384]{0:T(512)S(1)}) custom-call(bf16[128,384]{1,0:T(8,128)(2,1)} %x_in.1, f32[384]{0:T(512)} %gain_in.1, bf16[384,1536]{1,0:T(8,128)(2,1)} %w_in.1, bf16[128,1536]{1,0:T(8,128)(2,1)} %pre_in.1, bf16[128,1536]{1,0:T(8,128)(2,1)} %ga_in.1), custom_call_target="tpu_custom_call" | custom-call | tf_op jit(solution)/shard_map/pallas_call | solution.py:523
  102.9 1.4 %copy.11 = f32[384,1536]{1,0:T(8,128)} copy(f32[384,1536]{1,0:T(8,128)S(1)} %get-tuple-element.4) | data formatting | bytes 4718592
  104.3 0.6 copy.12
  104.9 0.6 copy.13

commit v5 on v4

--- a/solution.py
+++ b/solution.py
@@ -453,9 +453,9 @@
     for s in (1, -1):
         wait_sibling(1, zm(s))
         project(1, zm(s))
-    ring_step(1, 4, 0)
     gx[x] = gain_wait(gy, NY, yy, gy_send, gy_recv)
     gain_sum(gx, NX, x, gx_send, gx_recv, at_x)
+    ring_step(1, 4, 0)
     for s in (2, -2):
         wait_sibling(1, zm(s))
         project(1, zm(s))

time: 107 us -> 107 us (level)
  no operation moved by 1% of the time
where the time goes in v5:
time: 107 us; the launch traced here: 106 us
  Pallas kernels  102 us (95%)
  local copies, waits for them, and re-layouts  2.63 us (2%)
    pallas_call x1, Pallas kernels, shards(): pl.pallas_call(kernel, out_shape=(jax.ShapeDtypeStruct((ROWS, FEAT), BF16...  102 us
    unnamed x3, local copies, waits for them, and re-layouts  2.63 us

profile of v5, /device:TPU:1, one launch (start us, length us, event | category | flops | bytes accessed | tf_op | source)
XLA Modules:
  0.0 105.5 jit_solution(10617019345110497143)
XLA Ops:
  0.6 102.2 %shard_map.76 = (bf16[128,384]{1,0:T(8,128)(2,1)S(1)}, f32[384,1536]{1,0:T(8,128)S(1)}, f32[384]{0:T(512)S(1)}) custom-call(bf16[128,384]{1,0:T(8,128)(2,1)} %x_in.1, f32[384]{0:T(512)} %gain_in.1, bf16[384,1536]{1,0:T(8,128)(2,1)} %w_in.1, bf16[128,1536]{1,0:T(8,128)(2,1)} %pre_in.1, bf16[128,1536]{1,0:T(8,128)(2,1)} %ga_in.1), custom_call_target="tpu_custom_call" | custom-call | tf_op jit(solution)/shard_map/pallas_call | solution.py:523
  102.9 1.4 %copy.11 = f32[384,1536]{1,0:T(8,128)} copy(f32[384,1536]{1,0:T(8,128)S(1)} %get-tuple-element.4) | data formatting | bytes 4718592
  104.3 0.6 copy.12
  104.9 0.6 copy.13
